TPU v7x, 256 devices: a whole 4x4x8 slice. The times are simulated.
256 devices in a mesh: wide: 64 (over y, x_lo, z), narrow: 4 (over x_hi, core).
Axes of the slice: x: 4 (x_hi: 2, x_lo: 2; x = x_hi * 2 + x_lo), y: 4, z: 8, core: 2. Of those that a mesh axis runs over, the one named last changes fastest.
Arguments:
- gradient: bfloat16 [2560, 7168], P('wide', 'narrow'), may hold values from -6 to 6
- left_basis: bfloat16 [2560, 2560], P(None, 'narrow'), may hold values from -0.125 to 0.125
- right_basis: bfloat16 [7168, 7168], P('wide', 'narrow'), may hold values from -0.0625 to 0.0625
- first_moment: float32 [7168, 2560], P('wide', 'narrow'), may hold values from -0.6 to 0.6
- second_moment: float32 [7168, 2560], P('wide', 'narrow'), may hold values from 0.01 to 0.1
Outputs:
- update: float32 [2560, 7168], P('wide', 'narrow')
- new_first: float32 [7168, 2560], P('wide', 'narrow')
- new_second: float32 [7168, 2560], P('wide', 'narrow')
All inputs are finite; a program needn't handle non-finite values.
Results may differ from a plain program's by a relative error of at most 0.0038.
Values may be sent and summed in bfloat16 or wider, within the bound.
A program may use at most 64 MiB of HBM per device.

v0:
```python
import jax
import jax.numpy as jnp
from jax import lax
from jax.sharding import PartitionSpec as P

STEP = 10


beta_first = 0.9
beta_second = 0.95
epsilon = 1e-08


def narrow_total(partial_value):
    share = lax.psum_scatter(partial_value, "narrow", scatter_dimension=1, tiled=True).astype(
        jnp.bfloat16
    )
    return lax.all_gather(share, "narrow", axis=1, tiled=True)


def contract_first(left_side, right_side):
    return lax.dot_general(
        left_side, right_side, (((0,), (0,)), ((), ())), preferred_element_type=jnp.float32
    )


def body(gradient, left_basis, right_basis, first_moment, second_moment):
    partial_value = lax.dot_general(
        right_basis,
        lax.all_gather(gradient, "wide", axis=0, tiled=True),
        (((1,), (1,)), ((), ())),
        preferred_element_type=jnp.float32,
    )
    right_rotated = narrow_total(partial_value)
    rotated = jnp.dot(right_rotated, left_basis, preferred_element_type=jnp.float32)
    new_first = beta_first * first_moment + (1.0 - beta_first) * rotated
    new_second = beta_second * second_moment + (1.0 - beta_second) * rotated * rotated
    first_fix = 1.0 - beta_first**STEP
    second_fix = 1.0 - beta_second**STEP
    normalized = (new_first / first_fix / (jnp.sqrt(new_second / second_fix) + epsilon)).astype(
        jnp.bfloat16
    )
    left_partial = lax.dot_general(
        normalized, left_basis, (((1,), (1,)), ((), ())), preferred_element_type=jnp.float32
    )
    back_left = narrow_total(left_partial)
    full_term = contract_first(back_left, right_basis)
    column_part = lax.psum_scatter(full_term, "wide", scatter_dimension=1, tiled=True)
    update = lax.all_to_all(column_part, "wide", split_axis=0, concat_axis=1, tiled=True)
    return (update, new_first, new_second)


def solution(mesh):
    return jax.shard_map(
        body,
        mesh=mesh,
        in_specs=(
            P("wide", "narrow"),
            P(None, "narrow"),
            P("wide", "narrow"),
            P("wide", "narrow"),
            P("wide", "narrow"),
        ),
        out_specs=(P("wide", "narrow"), P("wide", "narrow"), P("wide", "narrow")),
        check_vma=False,
    )
```

profile of v0, /device:TPU:1, one launch (start us, length us, event | category | flops | bytes accessed | tf_op | source)
XLA Modules:
  0.0 827.6 jit_solution(12109436635512156272)
XLA Ops:
  8.0 284.3 %all-gather.2.cloned.1.call-done = bf16[2560,1792]{1,0:T(8,128)(2,1)} async-done(((bf16[40,1792]{1,0:T(8,128)(2,1)}), bf16[2560,1792]{1,0:T(8,128)(2,1)}) %all-gather.2.cloned.1.call-update) | async-done | bytes 9175056 | tf_op jit(solution)/shard_map/all_gather | solution.py:30
  292.3 7.7 fusion.9
  300.0 69.2 %reduce-scatter.5.cloned.1.call-done = f32[112,640]{1,0:T(8,128)} async-done(((f32[112,2560]{1,0:T(8,128)}), f32[112,640]{1,0:T(8,128)}) %reduce-scatter.5.cloned.1.call-update) | async-done | bytes 286736 | tf_op jit(solution)/shard_map/reduce_scatter | solution.py:15
  370.2 9.1 %all_gather.10 = bf16[112,2560]{1,0:T(8,128)(2,1)S(1)} all-gather(bf16[112,640]{1,0:T(8,128)(2,1)S(1)} %convert_element_type.9), channel_id=1, replica_groups=mesh['wide'=64,'narrow'=4] {'narrow'}, dimensions={1}, use_global_device_ids=true | all-gather | bytes 716800 | tf_op jit(solution)/shard_map/all_gather | solution.py:18
  384.0 36.7 %reduce-scatter.7.cloned.1.call-done = f32[112,640]{1,0:T(8,128)} async-done(((f32[112,2560]{1,0:T(8,128)}), f32[112,640]{1,0:T(8,128)}) %reduce-scatter.7.cloned.1.call-update) | async-done | bytes 286736 | tf_op jit(solution)/shard_map/reduce_scatter | solution.py:15
  421.7 9.1 %all_gather.11 = bf16[112,2560]{1,0:T(8,128)(2,1)S(1)} all-gather(bf16[112,640]{1,0:T(8,128)(2,1)S(1)} %convert_element_type.11), channel_id=1, replica_groups=mesh['wide'=64,'narrow'=4] {'narrow'}, dimensions={1}, use_global_device_ids=true | all-gather | bytes 716800 | tf_op jit(solution)/shard_map/all_gather | solution.py:18
  430.7 9.9 %fusion.10 = f32[2560,1792]{0,1:T(8,128)} fusion(bf16[112,2560]{1,0:T(8,128)(2,1)S(1)} %all_gather.11, bf16[112,1792]{1,0:T(8,128)(2,1)} %param.7), kind=kOutput, calls=%fused_computation.15 | convolution fusion | flops 1027604480 | bytes 19324928 | tf_op jit(solution)/shard_map/dot_general | solution.py:22
  440.6 235.6 %fusion = f32[2560,32]{0,1:T(8,128)} fusion(f32[2560,1792]{0,1:T(8,128)} %fusion.10), kind=kCustom, calls=%all-reduce-scatter | all-reduce-scatter fusion | flops 5242881 | bytes 18678784
  683.3 4.8 collective-permute-start.2
  688.1 7.3 collective-permute-start.3
  695.4 3.6 collective-permute-done.7
  703.1 4.9 collective-permute-start.6
  709.2 11.5 %collective-permute-done.3 = f32[2560,32]{0,1:T(8,128)} collective-permute-done((f32[2560,32]{0,1:T(8,128)}, f32[2560,32]{0,1:T(8,128)}, u32[]{:S(2)}, u32[]{:S(2)}) %collective-permute-start.3) | collective-permute-done | bytes 327712
  720.7 7.9 collective-permute-done.4
  728.6 15.2 %collective-permute-done.5 = f32[2560,32]{0,1:T(8,128)} collective-permute-done((f32[2560,32]{0,1:T(8,128)}, f32[2560,32]{0,1:T(8,128)}, u32[]{:S(2)}, u32[]{:S(2)}) %collective-permute-start.5) | collective-permute-done | bytes 327712
  743.7 7.8 collective-permute-done.6
  751.6 23.3 %concatenate = f32[2560,284]{0,1:T(8,128)} concatenate(f32[2560,28]{0,1:T(8,128)} %collective-permute-done.7, f32[2560,32]{0,1:T(8,128)} %collective-permute-done.6, f32[2560,32]{0,1:T(8,128)} %collective-permute-done.5, f32[2560,32]{0,1:T(8,128)} %collective-permute-done.4, f32[2560,32]{0,1:T(8,128)} %collective-permute-done.3, f32[2560,32]{0,1:T(8,128)} %collective-permute-done.2, ...), dimensions={1} | concatenate | bytes 5816320
  776.6 2.7 all_to_all.14
  779.3 2.7 copy.14
  782.0 2.8 reshape.11
  784.8 23.2 %all_to_all.19 = f32[64,1,1120]{2,1,0:T(1,128)} all-to-all(f32[64,1,1120]{2,1,0:T(1,128)} %reshape.11), channel_id=1, replica_groups=mesh['wide'=64,'narrow'=4] {'wide'}, dimensions={0} | all-to-all | bytes 573440 | tf_op jit(solution)/shard_map/all_to_all | solution.py:49
  808.6 3.1 reduce
  811.6 2.7 reshape.12
  816.6 2.3 reshape.9
  (32 shorter events, 25.9 us)
Async XLA Ops:
  7.2 372.1 %copy-start = (bf16[2560,640]{1,0:T(8,128)(2,1)S(1)}, bf16[2560,640]{1,0:T(8,128)(2,1)}, u32[]{:S(2)}) copy-start(bf16[2560,640]{1,0:T(8,128)(2,1)} %param.6) | copy-start | bytes 9830404
  7.2 285.1 %all-gather.2.cloned.1.call-start = ((), (), s32[]{:S(2)}) async-start(), calls=%async_computation.3 | async-start | bytes 9318400 | tf_op jit(solution)/shard_map/all_gather | solution.py:30
  7.9 361.3 %reduce-scatter.5.cloned.1.call-start = ((), (), s32[]{:S(2)}) async-start(), calls=%async_computation.4 | async-start | bytes 1433600 | tf_op jit(solution)/shard_map/reduce_scatter | solution.py:15
  300.0 120.7 %reduce-scatter.7.cloned.1.call-start = ((), (), s32[]{:S(2)}) async-start(), calls=%async_computation.5 | async-start | bytes 1433600 | tf_op jit(solution)/shard_map/reduce_scatter | solution.py:15
  381.0 0.7 copy-start.1
  381.0 0.8 copy-start.2
  440.6 267.4 %copy-start.3 = (u32[256]{0:T(256)S(1)}, u32[256]{0:T(256)}, u32[]{:S(2)}) copy-start(u32[256]{0:T(256)} %constant.22) | copy-start | bytes 3076
  676.2 24.8 %collective-permute-start = (f32[2560,32]{0,1:T(8,128)}, f32[2560,32]{0,1:T(8,128)}, u32[]{:S(2)}, u32[]{:S(2)}) collective-permute-start(f32[2560,32]{0,1:T(8,128)} %fusion), channel_id=1, source_target_pairs={{0,4},{4,8},{8,12},{12,16},{16,20},{20,24},{24,28},{28,32},{32,36}... | collective-permute-start | bytes 983048
  678.3 24.8 %collective-permute-start.1 = (f32[2560,32]{0,1:T(8,128)}, f32[2560,32]{0,1:T(8,128)}, u32[]{:S(2)}, u32[]{:S(2)}) collective-permute-start(f32[2560,32]{0,1:T(8,128)} %fusion), channel_id=1, source_target_pairs={{0,8},{4,12},{8,16},{12,20},{16,24},{20,28},{24,32},{28,36},{32,40... | collective-permute-start | bytes 983048
  681.3 17.7 %collective-permute-start.7 = (f32[2560,28]{0,1:T(8,128)S(1)}, f32[2560,28]{0,1:T(8,128)}, u32[]{:S(2)}, u32[]{:S(2)}) collective-permute-start(f32[2560,28]{0,1:T(8,128)S(1)} %slice), channel_id=1, source_target_pairs={{0,32},{4,36},{8,40},{12,44},{16,48},{20,52},{24,56},{28,60},{32,6... | collective-permute-start | bytes 860168
  683.3 25.9 %collective-permute-start.2 = (f32[2560,32]{0,1:T(8,128)}, f32[2560,32]{0,1:T(8,128)}, u32[]{:S(2)}, u32[]{:S(2)}) collective-permute-start(f32[2560,32]{0,1:T(8,128)} %fusion), channel_id=1, source_target_pairs={{0,12},{4,16},{8,20},{12,24},{16,28},{20,32},{24,36},{28,40},{32,4... | collective-permute-start | bytes 983048
  688.1 32.6 %collective-permute-start.3 = (f32[2560,32]{0,1:T(8,128)}, f32[2560,32]{0,1:T(8,128)}, u32[]{:S(2)}, u32[]{:S(2)}) collective-permute-start(f32[2560,32]{0,1:T(8,128)} %fusion), channel_id=1, source_target_pairs={{0,16},{4,20},{8,24},{12,28},{16,32},{20,36},{24,40},{28,44},{32,4... | collective-permute-start | bytes 983048
  699.0 29.5 %collective-permute-start.4 = (f32[2560,32]{0,1:T(8,128)}, f32[2560,32]{0,1:T(8,128)}, u32[]{:S(2)}, u32[]{:S(2)}) collective-permute-start(f32[2560,32]{0,1:T(8,128)} %fusion), channel_id=1, source_target_pairs={{0,20},{4,24},{8,28},{12,32},{16,36},{20,40},{24,44},{28,48},{32,5... | collective-permute-start | bytes 983048
  701.0 42.7 %collective-permute-start.5 = (f32[2560,32]{0,1:T(8,128)}, f32[2560,32]{0,1:T(8,128)}, u32[]{:S(2)}, u32[]{:S(2)}) collective-permute-start(f32[2560,32]{0,1:T(8,128)} %fusion), channel_id=1, source_target_pairs={{0,24},{4,28},{8,32},{12,36},{16,40},{20,44},{24,48},{28,52},{32,5... | collective-permute-start | bytes 983048
  703.1 48.5 %collective-permute-start.6 = (f32[2560,32]{0,1:T(8,128)}, f32[2560,32]{0,1:T(8,128)}, u32[]{:S(2)}, u32[]{:S(2)}) collective-permute-start(f32[2560,32]{0,1:T(8,128)} %fusion), channel_id=1, source_target_pairs={{0,28},{4,32},{8,36},{12,40},{16,44},{20,48},{24,52},{28,56},{32,6... | collective-permute-start | bytes 983048
Sparse Core Ops, SparseCore 0:
  9.8 282.4 all-gather.1
  300.1 69.0 reduce-scatter.4
  384.1 36.5 reduce-scatter.6
where the time goes:
time: 830 us; the launch traced here: 828 us
  waiting for transfers between devices  437 us (53%)
  blocking collectives  277 us (33%)
  local copies, waits for them, and re-layouts  45.6 us (5%)
  starting transfers between devices  27.2 us (3%)
  matrix products  21.4 us (3%)
  between operations  14.5 us (2%)
    all_gather x1, waiting for transfers between devices, body(): lax.all_gather(gradient, 'wide', axis=0, tiled=True)  284 us
    unnamed x1, blocking collectives  236 us
    reduce_scatter x2, waiting for transfers between devices, narrow_total(): lax.psum_scatter(partial_value, 'narrow', scatter_dimension=1, tiled=True)  106 us
    unnamed x11, waiting for transfers between devices  46.7 us
    unnamed x14, local copies, waits for them, and re-layouts  33 us
    unnamed x8, starting transfers between devices  27.1 us
    all_to_all x1, blocking collectives, body(): lax.all_to_all(column_part, 'wide', split_axis=0, concat_axis=1, tiled=True)  23.2 us
    all_gather x2, blocking collectives, narrow_total(): return lax.all_gather(share, 'narrow', axis=1, tiled=True)  18.1 us
  transfers between devices with their start and end apart: 11, of which 8 were waited for; matrix products, arithmetic and copies ran while one was open for 0% of the time, Pallas kernels for 0%

commit v1 on v0

v1 whole, which is shorter than its diff:
```python
import functools

import jax
import jax.numpy as jnp
from jax import lax
from jax.experimental import pallas as pl
from jax.experimental.pallas import tpu as pltpu
from jax.sharding import PartitionSpec as P

STEP = 10

beta_first = 0.9
beta_second = 0.95
epsilon = 1e-08

MESH = pl.DeviceIdType.MESH
BF16 = jnp.bfloat16
F32 = jnp.float32

NY, NXL, NZ = 4, 2, 8
GROUP = NY * NXL
GROWS = 40
ROWS = 112
COLS = 1792
EIG = 640
BLOCK = NZ * GROWS
HALF = COLS // 2
PART = 64
OFFSET = ROWS - PART
ORDER = ((0, 0), (0, 1), (1, 0), (3, 0), (2, 0), (1, 1), (3, 1), (2, 1))
TOP, LOW = (0, 64), (64, 48)


class Copies:
    def __init__(self, send_sem, recv_sem):
        self.send_sem, self.recv_sem, self.made = send_sem, recv_sem, {}

    def start(self, name, src, dst, device):
        at = len(self.made)
        copy = pltpu.make_async_remote_copy(
            src_ref=src,
            dst_ref=dst,
            send_sem=self.send_sem.at[at],
            recv_sem=self.recv_sem.at[at],
            device_id=device,
            device_id_type=MESH,
        )
        copy.start()
        self.made[name] = copy

    def wait(self, name):
        self.made[name].wait_recv()

    def finish(self):
        for copy in self.made.values():
            copy.wait_send()


def kernel(
    gradient, left_basis, right_basis, first_moment, second_moment,
    update, new_first, new_second,
    g_slots, g_wide, g_all, r_slots, left, first, second, first_out, second_out,
    forward, forward_got, forward_sent, forward_in, rotated_in,
    back, back_got, back_sent, back_in, back_left,
    total, sums, sums_in, update_out,
    local_sem, send_sem, recv_sem,
):
    wide, narrow = lax.axis_index("wide"), lax.axis_index("narrow")
    y, xl, z = wide // (NXL * NZ), lax.rem(wide // NZ, NXL), lax.rem(wide, NZ)
    xh, core = narrow // 2, lax.rem(narrow, 2)
    own = wide // NZ

    def member(dy, dxl):
        return lax.rem(y + dy, NY) * NXL + lax.rem(xl + dxl, NXL)

    def at(group=own, zz=z, hi=xh, cc=core):
        return {"wide": group * NZ + zz, "narrow": hi * 2 + cc}

    z_up, z_down = at(zz=lax.rem(z + 1, NZ)), at(zz=lax.rem(z + NZ - 1, NZ))
    y_up, y_down = at(group=member(1, 0)), at(group=member(3, 0))
    x_other = at(group=member(0, 1))
    sibling = at(cc=1 - core)
    hi_other = 1 - xh

    loads = [
        pltpu.make_async_copy(src, dst, local_sem.at[i])
        for i, (src, dst) in enumerate(
            (
                (gradient, g_slots.at[z]),
                (right_basis, r_slots.at[own]),
                (left_basis, left),
                (first_moment, first),
                (second_moment, second),
            )
        )
    ]
    for load in loads:
        load.start()

    barrier = pltpu.get_barrier_semaphore()
    peers = [z_up, z_down, sibling]
    for dy, dxl in ORDER:
        for hi in (xh, hi_other):
            if (dy, dxl) != (0, 0) or hi is not xh:
                peers.append(at(group=member(dy, dxl), hi=hi))
    for peer in peers:
        pl.semaphore_signal(barrier, inc=1, device_id=peer, device_id_type=MESH)
    pl.semaphore_wait(barrier, len(peers))

    copies = Copies(send_sem, recv_sem)

    def g_slot(distance):
        return g_slots.at[lax.rem(z + distance + NZ, NZ)]

    def g_piece(distance, half):
        return g_slots.at[lax.rem(z + distance + NZ, NZ), :, pl.ds(half * HALF, HALF)]

    def r_piece(dy, dxl, piece):
        return r_slots.at[member(dy, dxl), pl.ds(*piece), :]

    def send_r(name, dy, dxl, piece, device):
        ref = r_piece(dy, dxl, piece)
        copies.start(name, ref, ref, device)

    loads[0].wait()
    copies.start("g+1", g_slot(0), g_slot(0), z_up)
    copies.start("g-1", g_slot(0), g_slot(0), z_down)
    loads[1].wait()
    for tag, piece in (("t", TOP), ("l", LOW)):
        send_r("y+" + tag, 0, 0, piece, y_up)
        send_r("y-" + tag, 0, 0, piece, y_down)
        send_r("x" + tag, 0, 0, piece, x_other)
    for hop in (1,):
        copies.wait("g+1")
        copies.start("g+2", g_slot(-1), g_slot(-1), z_up)
        copies.wait("g-1")
        copies.start("g-2", g_slot(1), g_slot(1), z_down)
    copies.wait("y+t")
    send_r("yy+", 3, 0, TOP, y_up)
    send_r("xt3", 3, 0, TOP, x_other)
    copies.wait("y-t")
    send_r("xt1", 1, 0, TOP, x_other)
    copies.wait("g+2")
    copies.start("g+3", g_slot(-2), g_slot(-2), z_up)
    copies.wait("g-2")
    copies.start("g-3", g_slot(2), g_slot(2), z_down)
    copies.wait("y-l")
    send_r("yy-", 1, 0, LOW, y_down)
    copies.wait("xl")
    send_r("yx+", 0, 1, LOW, y_up)
    send_r("yx-", 0, 1, LOW, y_down)
    copies.wait("g+3")
    copies.start("g+4", g_piece(-3, 0), g_piece(-3, 0), z_up)
    copies.wait("g-3")
    copies.start("g-4", g_piece(3, 1), g_piece(3, 1), z_down)
    copies.wait("yx+")
    send_r("yxx+", 3, 1, LOW, y_up)
    copies.wait("xt1")
    send_r("yxx-", 1, 1, TOP, y_down)
    copies.wait("g+4")
    copies.wait("g-4")

    for i in range(NZ):
        g_wide[pl.ds(i * GROWS, GROWS), :] = g_slots[i].astype(F32)
    g_all[...] = g_wide[...].astype(BF16)

    needs = {
        (0, 0): (),
        (0, 1): ("xt",),
        (1, 0): (),
        (3, 0): ("y+l",),
        (2, 0): ("yy+", "yy-"),
        (1, 1): ("yx-",),
        (3, 1): ("xt3",),
        (2, 1): ("yxx+", "yxx-"),
    }

    mine = pl.ds(pl.multiple_of(core * OFFSET, 16), PART)
    theirs = pl.ds(pl.multiple_of((1 - core) * OFFSET, 16), PART)
    kept = pl.ds(pl.multiple_of(core * PART, 16), OFFSET)

    def give_core(tag, partial, got, group):
        copies.start(tag, partial.at[group, theirs, :], got.at[group], sibling)

    def spread(tag, partial, got, sent, landed):
        for dy, dxl in ORDER:
            group = member(dy, dxl)
            copies.wait(f"{tag}c{dy}{dxl}")
            sent[group] = (partial[group, mine, :] + got[group]).astype(BF16)
            for e, hi in ((0, xh), (1, hi_other)):
                if (dy, dxl, e) != (0, 0, 0):
                    copies.start(
                        f"{tag}s{dy}{dxl}{e}", sent.at[group], landed.at[e, own], at(group=group, hi=hi)
                    )

    def collect(tag, sent, landed, result):
        for dy, dxl in ORDER:
            source = member((NY - dy) % NY, dxl)
            if (dy, dxl) == (0, 0):
                here = sent[own]
            else:
                copies.wait(f"{tag}s{dy}{dxl}0")
                here = landed[0, source]
            copies.wait(f"{tag}s{dy}{dxl}1")
            result[source, mine, :] = (here.astype(F32) + landed[1, source].astype(F32)).astype(BF16)
            ref = result.at[source, kept, :]
            copies.start(f"{tag}r{dy}{dxl}", ref, ref, sibling)

    for dy, dxl in ORDER:
        for name in needs[(dy, dxl)]:
            copies.wait(name)
        group = member(dy, dxl)
        forward[group] = lax.dot_general(
            r_slots[group], g_all[...], (((1,), (1,)), ((), ())), preferred_element_type=F32
        )
        give_core(f"fc{dy}{dxl}", forward, forward_got, group)
    spread("f", forward, forward_got, forward_sent, forward_in)
    collect("f", forward_sent, forward_in, rotated_in)

    loads[2].wait()

    def left_rows(group):
        return left[pl.ds(pl.multiple_of(group * BLOCK, 64), BLOCK), :]

    rotated = jnp.zeros((ROWS, EIG), F32)
    for dy, dxl in ORDER:
        source = member((NY - dy) % NY, dxl)
        copies.wait(f"fr{dy}{dxl}")
        rotated += jnp.dot(rotated_in[source], left_rows(source), preferred_element_type=F32)

    loads[3].wait()
    loads[4].wait()
    next_first = beta_first * first[...] + (1.0 - beta_first) * rotated
    next_second = beta_second * second[...] + (1.0 - beta_second) * rotated * rotated
    first_out[...] = next_first
    second_out[...] = next_second
    stores = [
        pltpu.make_async_copy(first_out, new_first, local_sem.at[5]),
        pltpu.make_async_copy(second_out, new_second, local_sem.at[6]),
    ]
    for store in stores:
        store.start()
    first_fix = 1.0 - beta_first**STEP
    second_fix = 1.0 - beta_second**STEP
    normalized = (next_first / first_fix / (jnp.sqrt(next_second / second_fix) + epsilon)).astype(BF16)

    for dy, dxl in ORDER:
        group = member(dy, dxl)
        back[group] = lax.dot_general(
            normalized, left_rows(group), (((1,), (1,)), ((), ())), preferred_element_type=F32
        )
        give_core(f"bc{dy}{dxl}", back, back_got, group)
    spread("b", back, back_got, back_sent, back_in)
    collect("b", back_sent, back_in, back_left)
    for dy, dxl in ORDER:
        copies.wait(f"br{dy}{dxl}")

    total[...] = lax.dot_general(
        back_left[...].reshape(GROUP * ROWS, BLOCK),
        r_slots[...].reshape(GROUP * ROWS, COLS),
        (((0,), (0,)), ((), ())),
        preferred_element_type=F32,
    )

    def total_rows(distance, half):
        rows = lax.rem(z + distance + NZ, NZ) * GROWS
        return total[pl.ds(pl.multiple_of(rows, 8), GROWS), pl.ds(half * HALF, HALF)]

    for step in range(4):
        for way, sign, device in ((0, -1, z_down), (1, 1, z_up)):
            for half in (0, 1):
                if step == 0 and half != way:
                    continue
                value = total_rows(sign * (4 - step), half)
                if step > 1 or (step == 1 and half == way):
                    copies.wait(f"u{step - 1}{way}{half}")
                    value = value + sums_in[way, step - 1, half]
                sums[way, step, half] = value
                copies.start(f"u{step}{way}{half}", sums.at[way, step, half], sums_in.at[way, step, half], device)
    for half in (0, 1):
        value = total_rows(0, half)
        for way in (0, 1):
            copies.wait(f"u3{way}{half}")
            value = value + sums_in[way, 3, half]
        update_out[:, pl.ds(half * HALF, HALF)] = value
    last = pltpu.make_async_copy(update_out, update, local_sem.at[7])
    last.start()
    last.wait()
    for store in stores:
        store.wait()
    copies.finish()


COPIES = 8 + 14 + 2 * (8 + 15 + 8) + 14


def body(gradient, left_basis, right_basis, first_moment, second_moment):
    partials = [
        pltpu.VMEM((GROUP, ROWS, BLOCK), F32),
        pltpu.VMEM((GROUP, PART, BLOCK), F32),
        pltpu.VMEM((GROUP, PART, BLOCK), BF16),
        pltpu.VMEM((2, GROUP, PART, BLOCK), BF16),
        pltpu.VMEM((GROUP, ROWS, BLOCK), BF16),
    ]
    moment = pltpu.VMEM((ROWS, EIG), F32)
    return pl.pallas_call(
        kernel,
        out_shape=(
            jax.ShapeDtypeStruct((GROWS, COLS), F32),
            jax.ShapeDtypeStruct((ROWS, EIG), F32),
            jax.ShapeDtypeStruct((ROWS, EIG), F32),
        ),
        in_specs=[pl.BlockSpec(memory_space=pl.ANY)] * 5,
        out_specs=[pl.BlockSpec(memory_space=pl.ANY)] * 3,
        scratch_shapes=[
            pltpu.VMEM((NZ, GROWS, COLS), BF16),
            pltpu.VMEM((BLOCK, COLS), F32),
            pltpu.VMEM((BLOCK, COLS), BF16),
            pltpu.VMEM((GROUP, ROWS, COLS), BF16),
            pltpu.VMEM((GROUP * BLOCK, EIG), BF16),
            moment,
            moment,
            moment,
            moment,
            *partials,
            *partials,
            pltpu.VMEM((BLOCK, COLS), F32),
            pltpu.VMEM((2, 4, 2, GROWS, HALF), F32),
            pltpu.VMEM((2, 4, 2, GROWS, HALF), F32),
            pltpu.VMEM((GROWS, COLS), F32),
            pltpu.SemaphoreType.DMA((8,)),
            pltpu.SemaphoreType.DMA((COPIES,)),
            pltpu.SemaphoreType.DMA((COPIES,)),
        ],
        compiler_params=pltpu.CompilerParams(
            collective_id=0, has_side_effects=True, vmem_limit_bytes=56 * 1024 * 1024
        ),
        cost_estimate=pl.CostEstimate(flops=3 * 10**9, bytes_accessed=5 * 10**6, transcendentals=0),
    )(gradient, left_basis, right_basis, first_moment, second_moment)


def solution(mesh):
    return jax.shard_map(
        body,
        mesh=mesh,
        in_specs=(
            P("wide", "narrow"),
            P(None, "narrow"),
            P("wide", "narrow"),
            P("wide", "narrow"),
            P("wide", "narrow"),
        ),
        out_specs=(P("wide", "narrow"), P("wide", "narrow"), P("wide", "narrow")),
        check_vma=False,
    )
```

time: 830 us -> 99.9 us (0.12)
  waiting for transfers between devices: 437 us -> 0 us
  blocking collectives: 277 us -> 0 us
  Pallas kernels: 0 us -> 93.2 us
  local copies, waits for them, and re-layouts: 45.6 us -> 5.06 us
  starting transfers between devices: 27.2 us -> 0 us
  matrix products: 21.4 us -> 0 us
  between operations: 14.5 us -> 0.64 us
    all_gather x1 -> x0, waiting for transfers between devices: 284 us -> none  [body(): lax.all_gather(gradient, 'wide', axis=0, tiled=True)]
    unnamed x1 -> x0, blocking collectives: 236 us -> none
    reduce_scatter x2 -> x0, waiting for transfers between devices: 106 us -> none  [narrow_total(): lax.psum_scatter(partial_value, 'narrow', scatter_dimension=1, tiled=True)]
    pallas_call x0 -> x1, Pallas kernels: none -> 93.2 us  [body(): pl.pallas_call(kernel, out_shape=(jax.ShapeDtypeStruct((GROWS, COLS), F32...]
    unnamed x11 -> x0, waiting for transfers between devices: 46.7 us -> none
    unnamed x14 -> x3, local copies, waits for them, and re-layouts: 33 us -> 5.06 us
    unnamed x8 -> x0, starting transfers between devices: 27.1 us -> none
    all_to_all x1 -> x0, blocking collectives: 23.2 us -> none  [body(): lax.all_to_all(column_part, 'wide', split_axis=0, concat_axis=1, tiled=True)]
  transfers between devices with their start and end apart: 11 -> 0, of which waited for: 8 -> 0; matrix products, arithmetic and copies ran while one was open for 0% -> 0% of each run, Pallas kernels for 0% -> 0%
where the time goes in v1:
time: 99.9 us; the launch traced here: 98.9 us
  Pallas kernels  93.2 us (93%)
  local copies, waits for them, and re-layouts  5.06 us (5%)
    pallas_call x1, Pallas kernels, body(): pl.pallas_call(kernel, out_shape=(jax.ShapeDtypeStruct((GROWS, COLS), F32...  93.2 us
    unnamed x3, local copies, waits for them, and re-layouts  5.06 us

profile of v1, /device:TPU:1, one launch (start us, length us, event | category | flops | bytes accessed | tf_op | source)
XLA Modules:
  0.0 98.9 jit_solution(12920121322429297523)
XLA Ops:
  0.6 93.2 %shard_map.76 = (f32[40,1792]{1,0:T(8,128)}, f32[112,640]{1,0:T(8,128)}, f32[112,640]{1,0:T(8,128)}) custom-call(bf16[40,1792]{1,0:T(8,128)(2,1)} %gradient.1, bf16[2560,640]{1,0:T(8,128)(2,1)} %left_basis.1, bf16[112,1792]{1,0:T(8,128)(2,1)} %right_basis.1, f32[112,640]{1,0:T(8,128)} %first_moment.1, f32[112,640]{1,0:T(8,128)} %second_moment.1), custom_call_target="tpu_custom_call" | custom-call | flops 3000000000 | bytes 5000000 | tf_op jit(solution)/shard_map/pallas_call | solution.py:306
  93.9 1.7 %copy.11 = f32[40,1792]{1,0:T(8,128)} copy(f32[40,1792]{1,0:T(8,128)} %get-tuple-element.6) | data formatting | bytes 573440
  95.5 1.7 %copy.12 = f32[112,640]{1,0:T(8,128)} copy(f32[112,640]{1,0:T(8,128)} %get-tuple-element.7) | data formatting | bytes 573440
  97.2 1.7 %copy.13 = f32[112,640]{1,0:T(8,128)} copy(f32[112,640]{1,0:T(8,128)} %get-tuple-element.8) | data formatting | bytes 573440

commit v2 on v0

v2 whole, which is shorter than its diff:
```python
import jax
import jax.numpy as jnp
from jax import lax
from jax.experimental import pallas as pl
from jax.experimental.pallas import tpu as pltpu
from jax.sharding import PartitionSpec as P

STEP = 10

beta_first = 0.9
beta_second = 0.95
epsilon = 1e-08

MESH = pl.DeviceIdType.MESH
BF16 = jnp.bfloat16
F32 = jnp.float32

NY, NXL, NZ = 4, 2, 8
GROUP = NY * NXL
GROWS = 40
ROWS = 112
COLS = 1792
EIG = 640
BLOCK = NZ * GROWS
HALF = COLS // 2
BANDS = ((0, 64), (64, 48))
PIECES = (((0, 32), (32, 32)), ((0, 32), (32, 16)))
SPREAD = ((2, 1), (2, 0), (1, 1), (3, 1), (1, 0), (3, 0), (0, 1), (0, 0))
STRIPS = ((0, 256), (256, 256), (512, 384), (896, 256), (1152, 256), (1408, 384))


class Copies:
    def __init__(self, send_sem, recv_sem, local_sem):
        self.send_sem, self.recv_sem, self.local_sem = send_sem, recv_sem, local_sem
        self.made, self.here, self.waited = {}, {}, set()

    def start(self, name, src, dst, device):
        at = len(self.made)
        copy = pltpu.make_async_remote_copy(
            src_ref=src,
            dst_ref=dst,
            send_sem=self.send_sem.at[at],
            recv_sem=self.recv_sem.at[at],
            device_id=device,
            device_id_type=MESH,
        )
        copy.start()
        self.made[name] = copy

    def local(self, name, src, dst):
        copy = pltpu.make_async_copy(src, dst, self.local_sem.at[len(self.here)])
        copy.start()
        self.here[name] = copy

    def wait(self, *names):
        for name in names:
            if name not in self.waited:
                self.waited.add(name)
                if name in self.here:
                    self.here[name].wait()
                else:
                    self.made[name].wait_recv()

    def finish(self):
        self.wait(*self.here, *self.made)
        for copy in self.made.values():
            copy.wait_send()


def kernel(
    gradient, left_basis, right_basis, first_moment, second_moment,
    update, new_first, new_second,
    g_slots, g_wide, g_all, r_top, r_low, left, first, second, first_out, second_out,
    partial_top, partial_low, got_top, got_low, sent_top, sent_low, mid_top, mid_low,
    back_top, back_low, bgot_top, bgot_low, bsent_top, bsent_low, end_top, end_low,
    total, sums, sums_in, update_out,
    local_sem, send_sem, recv_sem,
):
    wide, narrow = lax.axis_index("wide"), lax.axis_index("narrow")
    y, xl, z = wide // (NXL * NZ), lax.rem(wide // NZ, NXL), lax.rem(wide, NZ)
    xh, core = narrow // 2, lax.rem(narrow, 2)
    own = wide // NZ

    def member(dy, dxl):
        return lax.rem(y + dy, NY) * NXL + lax.rem(xl + dxl, NXL)

    def source_of(dy, dxl):
        return member((NY - dy) % NY, dxl)

    def at(group=own, zz=z, hi=xh, cc=core):
        return {"wide": group * NZ + zz, "narrow": hi * 2 + cc}

    z_up, z_down = at(zz=lax.rem(z + 1, NZ)), at(zz=lax.rem(z + NZ - 1, NZ))
    y_up, y_down = at(group=member(1, 0)), at(group=member(3, 0))
    x_other = at(group=member(0, 1))
    sibling = at(cc=1 - core)
    target_hi = lax.rem(xh + core, 2)

    def target(dy, dxl):
        if (dy, dxl) == (0, 0):
            return at(hi=1 - xh)
        return at(group=member(dy, dxl), hi=target_hi)

    r_bands = (r_top, r_low)
    copies = Copies(send_sem, recv_sem, local_sem)
    for band, (first_row, rows) in enumerate(BANDS):
        copies.local(f"r{band}", right_basis.at[pl.ds(first_row, rows), :], r_bands[band].at[own])
    copies.local("g", gradient, g_slots.at[z])
    copies.local("left", left_basis, left)
    copies.local("first", first_moment, first)
    copies.local("second", second_moment, second)

    barrier = pltpu.get_barrier_semaphore()
    peers = [z_up, z_down, y_up, y_down, x_other, sibling] + [target(*d) for d in SPREAD]
    for peer in peers:
        pl.semaphore_signal(barrier, inc=1, device_id=peer, device_id_type=MESH)
    pl.semaphore_wait(barrier, len(peers))

    def send_g(hop, half):
        for way, sign, device in ((0, 1, z_up), (1, -1, z_down)):
            if hop < 3 or half == way:
                ref = g_slots.at[lax.rem(z - sign * hop + NZ, NZ), :, pl.ds(half * HALF, HALF)]
                copies.start(f"g{hop}{half}{way}", ref, ref, device)

    def pass_g(hop, half):
        for way in (0, 1):
            if hop < 3 or half == way:
                copies.wait(f"g{hop - 1}{half}{way}")
        send_g(hop, half)

    routes = {
        "+0": ((0, 0), 0, y_up, None),
        "+1": ((0, 0), 1, y_up, None),
        "-0": ((0, 0), 0, y_down, None),
        "-1": ((0, 0), 1, y_down, None),
        "x0": ((0, 0), 0, x_other, None),
        "x1": ((0, 0), 1, x_other, None),
        "++": ((3, 0), 0, y_up, "+0"),
        "--": ((1, 0), 1, y_down, "-1"),
        "fx1": ((1, 0), 0, x_other, "-0"),
        "fx3": ((3, 0), 0, x_other, "+0"),
        "y+": ((0, 1), 1, y_up, "x1"),
        "y-": ((0, 1), 1, y_down, "x1"),
        "y++": ((3, 1), 1, y_up, "y+"),
        "y--": ((1, 1), 0, y_down, "fx1"),
    }

    def pass_r(band, *names):
        for name in names:
            block, piece, device, after = routes[name]
            copies.wait(f"r{band}" if after is None else f"r{band}{after}")
            ref = r_bands[band].at[member(*block), pl.ds(*PIECES[band][piece]), :]
            copies.start(f"r{band}{name}", ref, ref, device)

    send_own = pass_r

    def compact(distance):
        slot = lax.rem(z + distance + NZ, NZ)
        g_wide[pl.ds(pl.multiple_of(slot * GROWS, 8), GROWS), :] = g_slots[slot].astype(F32)

    copies.wait("g")
    send_g(0, 0)
    send_g(0, 1)
    send_own(0, "+0", "-0", "x1", "+1", "-1", "x0")
    compact(0)
    pass_g(1, 0)
    pass_r(0, "++", "fx1", "y+", "y-", "fx3")
    send_own(1, "+0", "-0", "x1")
    pass_g(1, 1)
    send_own(1, "+1", "-1", "x0")
    pass_r(0, "--")
    compact(1)
    compact(-1)
    pass_g(2, 0)
    pass_g(2, 1)
    pass_r(0, "y--")
    compact(2)
    compact(-2)
    pass_g(3, 0)
    pass_r(0, "y++")
    pass_r(1, "fx1", "y+", "y-")
    pass_g(3, 1)
    pass_r(1, "--", "++", "fx3")
    copies.wait("g201", "g210")
    compact(3)
    compact(-3)
    copies.wait("g300", "g311")
    compact(4)
    g_all[...] = g_wide[...].astype(BF16)

    def left_rows(group):
        return left[pl.ds(pl.multiple_of(group * BLOCK, 64), BLOCK), :]

    def give_core(tag, band, i, partial, got, slots):
        copies.start(f"{tag}{band}c{i}", partial.at[slots], got.at[slots], sibling)

    def right_products(band, partial, got):
        rows = BANDS[band][1]
        copies.wait(*(f"r{band}{name}" for name in routes))
        for i in (0, 1):
            slots = pl.ds(i * GROUP // 2, GROUP // 2)
            right = r_bands[band][slots].reshape(GROUP // 2 * rows, COLS)
            partial[slots] = lax.dot_general(
                right, g_all[...], (((1,), (1,)), ((), ())), preferred_element_type=F32
            ).reshape(GROUP // 2, rows, BLOCK)
            give_core("f", band, i, partial, got, slots)

    def spread(tag, band, i, partial, got, sent, landed):
        d = SPREAD[i]
        group = member(*d)
        value = (partial[group] + got[group]).astype(BF16)
        sent[group] = value
        copies.start(f"{tag}{band}s{d}", sent.at[group], landed.at[0, own], target(*d))
        if d == (0, 0):
            landed[1, own] = value

    def spread_right(band, partial, got, sent, landed):
        copies.wait(f"f{band}c0", f"f{band}c1")
        for i in range(GROUP):
            spread("f", band, i, partial, got, sent, landed)

    def left_products(band, normalized, partial, got, sent, landed):
        for i in range(GROUP + 2):
            if i < GROUP:
                group = member(*SPREAD[i])
                partial[group] = lax.dot_general(
                    normalized, left_rows(group), (((1,), (1,)), ((), ())), preferred_element_type=F32
                )
                give_core("b", band, i, partial, got, group)
            if i >= 2:
                copies.wait(f"b{band}c{i - 2}")
                spread("b", band, i - 2, partial, got, sent, landed)

    def share(tag, band, landed):
        for d in SPREAD:
            source = source_of(*d)
            copies.wait(f"{tag}{band}s{d}")
            if d != (0, 0):
                copies.start(f"{tag}{band}r{d}", landed.at[0, source], landed.at[1, source], sibling)

    def await_share(tag, band, d):
        if d != (0, 0):
            copies.wait(f"{tag}{band}r{d}")

    first_fix = 1.0 - beta_first**STEP
    second_fix = 1.0 - beta_second**STEP

    def middle(band, landed):
        first_row, rows = BANDS[band]
        product = jnp.zeros((2 * rows, EIG), F32)
        for d in SPREAD:
            source = source_of(*d)
            await_share("f", band, d)
            product += jnp.dot(
                landed[:, source].reshape(2 * rows, BLOCK), left_rows(source), preferred_element_type=F32
            )
        rotated = product[:rows] + product[rows:]
        at_rows = pl.ds(first_row, rows)
        copies.wait("first", "second")
        next_first = beta_first * first[at_rows, :] + (1.0 - beta_first) * rotated
        next_second = beta_second * second[at_rows, :] + (1.0 - beta_second) * rotated * rotated
        first_out[at_rows, :] = next_first
        second_out[at_rows, :] = next_second
        return (next_first / first_fix / (jnp.sqrt(next_second / second_fix) + epsilon)).astype(BF16)

    def update_part(band, landed, half):
        rows = BANDS[band][1]
        right = r_bands[band][:, :, pl.ds(half * HALF, HALF)].reshape(GROUP * rows, HALF)
        return sum(
            lax.dot_general(
                landed[i].reshape(GROUP * rows, BLOCK),
                right,
                (((0,), (0,)), ((), ())),
                preferred_element_type=F32,
            )
            for i in (0, 1)
        )

    pass_r(1, "y--")
    right_products(0, partial_top, got_top)
    pass_r(1, "y++")
    spread_right(0, partial_top, got_top, sent_top, mid_top)
    right_products(1, partial_low, got_low)
    spread_right(1, partial_low, got_low, sent_low, mid_low)
    share("f", 0, mid_top)
    copies.wait("left")
    normalized = middle(0, mid_top)
    left_products(0, normalized, back_top, bgot_top, bsent_top, end_top)
    share("f", 1, mid_low)
    normalized = middle(1, mid_low)
    left_products(1, normalized, back_low, bgot_low, bsent_low, end_low)
    copies.local("new_first", first_out, new_first)
    copies.local("new_second", second_out, new_second)
    share("b", 0, end_top)
    for d in SPREAD:
        await_share("b", 0, d)
    for half in (0, 1):
        total[:, pl.ds(half * HALF, HALF)] = update_part(0, end_top, half)
    share("b", 1, end_low)
    for d in SPREAD:
        await_share("b", 1, d)
    for half in (0, 1):
        total[:, pl.ds(half * HALF, HALF)] += update_part(1, end_low, half)

    def total_rows(distance, strip):
        rows = lax.rem(z + distance + NZ, NZ) * GROWS
        return total[pl.ds(pl.multiple_of(rows, 8), GROWS), pl.ds(*STRIPS[strip])]

    for step in range(4):
        for strip in (0, 3, 1, 4, 2, 5):
            for way, sign, device in ((0, -1, z_down), (1, 1, z_up)):
                starts = strip // 3 == way
                if step == 0 and not starts:
                    continue
                columns = pl.ds(*STRIPS[strip])
                value = total_rows(sign * (4 - step), strip)
                if step > 1 or (step == 1 and starts):
                    copies.wait(f"u{step - 1}{way}{strip}")
                    value = value + sums_in[way, step - 1, :, columns].astype(F32)
                sums[way, step, :, columns] = value.astype(BF16)
                copies.start(
                    f"u{step}{way}{strip}",
                    sums.at[way, step, :, columns],
                    sums_in.at[way, step, :, columns],
                    device,
                )
    for strip in (0, 3, 1, 4, 2, 5):
        columns = pl.ds(*STRIPS[strip])
        value = total_rows(0, strip)
        for way in (0, 1):
            copies.wait(f"u3{way}{strip}")
            value = value + sums_in[way, 3, :, columns].astype(F32)
        update_out[:, columns] = value
    copies.local("update", update_out, update)
    copies.finish()


COPIES = 14 + 28 + 2 * (2 + 8 + 7) + 2 * (8 + 8 + 7) + 42


def body(gradient, left_basis, right_basis, first_moment, second_moment):
    def bands(*shape, dtype):
        return [pltpu.VMEM((*shape, rows, BLOCK), dtype) for _, rows in BANDS]

    middle = [
        *bands(GROUP, dtype=F32),
        *bands(GROUP, dtype=F32),
        *bands(GROUP, dtype=BF16),
        *bands(2, GROUP, dtype=BF16),
    ]
    moment = pltpu.VMEM((ROWS, EIG), F32)
    return pl.pallas_call(
        kernel,
        out_shape=(
            jax.ShapeDtypeStruct((GROWS, COLS), F32),
            jax.ShapeDtypeStruct((ROWS, EIG), F32),
            jax.ShapeDtypeStruct((ROWS, EIG), F32),
        ),
        in_specs=[pl.BlockSpec(memory_space=pl.ANY)] * 5,
        out_specs=[pl.BlockSpec(memory_space=pl.ANY)] * 3,
        scratch_shapes=[
            pltpu.VMEM((NZ, GROWS, COLS), BF16),
            pltpu.VMEM((BLOCK, COLS), F32),
            pltpu.VMEM((BLOCK, COLS), BF16),
            *(pltpu.VMEM((GROUP, rows, COLS), BF16) for _, rows in BANDS),
            pltpu.VMEM((GROUP * BLOCK, EIG), BF16),
            *[moment] * 4,
            *middle,
            *middle,
            pltpu.VMEM((BLOCK, COLS), F32),
            pltpu.VMEM((2, 4, GROWS, COLS), BF16),
            pltpu.VMEM((2, 4, GROWS, COLS), BF16),
            pltpu.VMEM((GROWS, COLS), F32),
            pltpu.SemaphoreType.DMA((9,)),
            pltpu.SemaphoreType.DMA((COPIES,)),
            pltpu.SemaphoreType.DMA((COPIES,)),
        ],
        compiler_params=pltpu.CompilerParams(
            collective_id=0, has_side_effects=True, vmem_limit_bytes=56 * 1024 * 1024
        ),
        cost_estimate=pl.CostEstimate(flops=3 * 10**9, bytes_accessed=5 * 10**6, transcendentals=0),
    )(gradient, left_basis, right_basis, first_moment, second_moment)


def solution(mesh):
    return jax.shard_map(
        body,
        mesh=mesh,
        in_specs=(
            P("wide", "narrow"),
            P(None, "narrow"),
            P("wide", "narrow"),
            P("wide", "narrow"),
            P("wide", "narrow"),
        ),
        out_specs=(P("wide", "narrow"), P("wide", "narrow"), P("wide", "narrow")),
        check_vma=False,
    )
```

time: 830 us -> 84.4 us (0.10)
  waiting for transfers between devices: 437 us -> 0 us
  blocking collectives: 277 us -> 0 us
  Pallas kernels: 0 us -> 78.6 us
  local copies, waits for them, and re-layouts: 45.6 us -> 5.06 us
  starting transfers between devices: 27.2 us -> 0 us
  matrix products: 21.4 us -> 0 us
  between operations: 14.5 us -> 0.64 us
    all_gather x1 -> x0, waiting for transfers between devices: 284 us -> none  [body(): lax.all_gather(gradient, 'wide', axis=0, tiled=True)]
    unnamed x1 -> x0, blocking collectives: 236 us -> none
    reduce_scatter x2 -> x0, waiting for transfers between devices: 106 us -> none  [narrow_total(): lax.psum_scatter(partial_value, 'narrow', scatter_dimension=1, tiled=True)]
    pallas_call x0 -> x1, Pallas kernels: none -> 78.6 us  [body(): pl.pallas_call(kernel, out_shape=(jax.ShapeDtypeStruct((GROWS, COLS), F32...]
    unnamed x11 -> x0, waiting for transfers between devices: 46.7 us -> none
    unnamed x14 -> x3, local copies, waits for them, and re-layouts: 33 us -> 5.06 us
    unnamed x8 -> x0, starting transfers between devices: 27.1 us -> none
    all_to_all x1 -> x0, blocking collectives: 23.2 us -> none  [body(): lax.all_to_all(column_part, 'wide', split_axis=0, concat_axis=1, tiled=True)]
  transfers between devices with their start and end apart: 11 -> 0, of which waited for: 8 -> 0; matrix products, arithmetic and copies ran while one was open for 0% -> 0% of each run, Pallas kernels for 0% -> 0%
where the time goes in v2:
time: 84.4 us; the launch traced here: 84.3 us
  Pallas kernels  78.6 us (93%)
  local copies, waits for them, and re-layouts  5.06 us (6%)
    pallas_call x1, Pallas kernels, body(): pl.pallas_call(kernel, out_shape=(jax.ShapeDtypeStruct((GROWS, COLS), F32...  78.6 us
    unnamed x3, local copies, waits for them, and re-layouts  5.06 us

profile of v2, /device:TPU:1, one launch (start us, length us, event | category | flops | bytes accessed | tf_op | source)
XLA Modules:
  0.0 84.3 jit_solution(3020066130272137048)
XLA Ops:
  0.6 78.6 %shard_map.76 = (f32[40,1792]{1,0:T(8,128)}, f32[112,640]{1,0:T(8,128)}, f32[112,640]{1,0:T(8,128)}) custom-call(bf16[40,1792]{1,0:T(8,128)(2,1)} %gradient.1, bf16[2560,640]{1,0:T(8,128)(2,1)} %left_basis.1, bf16[112,1792]{1,0:T(8,128)(2,1)} %right_basis.1, f32[112,640]{1,0:T(8,128)} %first_moment.1, f32[112,640]{1,0:T(8,128)} %second_moment.1), custom_call_target="tpu_custom_call" | custom-call | flops 3000000000 | bytes 5000000 | tf_op jit(solution)/shard_map/pallas_call | solution.py:352
  79.2 1.7 %copy.11 = f32[40,1792]{1,0:T(8,128)} copy(f32[40,1792]{1,0:T(8,128)} %get-tuple-element.6) | data formatting | bytes 573440
  80.9 1.7 %copy.12 = f32[112,640]{1,0:T(8,128)} copy(f32[112,640]{1,0:T(8,128)} %get-tuple-element.7) | data formatting | bytes 573440
  82.6 1.7 %copy.13 = f32[112,640]{1,0:T(8,128)} copy(f32[112,640]{1,0:T(8,128)} %get-tuple-element.8) | data formatting | bytes 573440

commit v3 on v2

v3 whole, which is shorter than its diff:
```python
import jax
import jax.numpy as jnp
from jax import lax
from jax.experimental import pallas as pl
from jax.experimental.pallas import tpu as pltpu
from jax.sharding import PartitionSpec as P

STEP = 10

beta_first = 0.9
beta_second = 0.95
epsilon = 1e-08

MESH = pl.DeviceIdType.MESH
BF16 = jnp.bfloat16
F32 = jnp.float32

NY, NXL, NZ = 4, 2, 8
GROUP = NY * NXL
GROWS = 40
ROWS = 112
COLS = 1792
EIG = 640
BLOCK = NZ * GROWS
HALF = COLS // 2
BANDS = ((0, 64), (64, 48))
PIECES = (((0, 32), (32, 32)), ((0, 32), (32, 16)))
FAR_FIRST = (2, 1, 3, 0)
SPREAD = tuple((dy, e) for dy in FAR_FIRST for e in (1, 0))
G_STRIPS = ((0, 384), (384, 512), (896, 384), (1280, 512))
STRIPS = ((0, 256), (256, 256), (512, 384), (896, 256), (1152, 256), (1408, 384))


class Copies:
    def __init__(self, send_sem, recv_sem, local_sem):
        self.send_sem, self.recv_sem, self.local_sem = send_sem, recv_sem, local_sem
        self.made, self.here, self.waited = {}, {}, set()

    def start(self, name, src, dst, device, only=None):
        at = len(self.made)
        copy = pltpu.make_async_remote_copy(
            src_ref=src,
            dst_ref=dst,
            send_sem=self.send_sem.at[at],
            recv_sem=self.recv_sem.at[at],
            device_id=device,
            device_id_type=MESH,
        )
        self.made[name] = copy, (lambda act: act()) if only is None else pl.when(only)
        self.made[name][1](copy.start)

    def local(self, name, src, dst):
        copy = pltpu.make_async_copy(src, dst, self.local_sem.at[len(self.here)])
        copy.start()
        self.here[name] = copy

    def wait(self, *names):
        for name in names:
            if name not in self.waited:
                self.waited.add(name)
                if name in self.here:
                    self.here[name].wait()
                else:
                    copy, where = self.made[name]
                    where(copy.wait_recv)

    def finish(self):
        self.wait(*self.here, *self.made)
        for copy, where in self.made.values():
            where(copy.wait_send)


def kernel(
    gradient, left_basis, right_basis, first_moment, second_moment,
    update, new_first, new_second,
    g_slots, g_wide, g_all, r_top, r_low, left, first, second, first_out, second_out,
    keep_top, keep_low, give_top, give_low, got_top, got_low, sent_top, sent_low, mid_top, mid_low,
    bkeep_top, bkeep_low, bgive_top, bgive_low, bgot_top, bgot_low, bsent_top, bsent_low, end_top, end_low,
    total, sums, sums_in, update_out,
    local_sem, send_sem, recv_sem,
):
    wide, narrow = lax.axis_index("wide"), lax.axis_index("narrow")
    y, xl, z = wide // (NXL * NZ), lax.rem(wide // NZ, NXL), lax.rem(wide, NZ)
    xh, core = narrow // 2, lax.rem(narrow, 2)
    own = wide // NZ

    def member(dy, dxl):
        return lax.rem(y + dy, NY), lax.rem(xl + dxl, NXL)

    def at(group=(y, xl), zz=z, hi=xh, cc=core):
        return {"wide": (group[0] * NXL + group[1]) * NZ + zz, "narrow": hi * 2 + cc}

    z_up, z_down = at(zz=lax.rem(z + 1, NZ)), at(zz=lax.rem(z + NZ - 1, NZ))
    y_up, y_down = at(group=member(1, 0)), at(group=member(3, 0))
    x_other = at(group=member(0, 1))
    sibling = at(cc=1 - core)

    def target(dy, e):
        return at(group=member(dy, core), hi=lax.rem(xh + e, 2))

    r_bands = (r_top, r_low)
    copies = Copies(send_sem, recv_sem, local_sem)
    for band, (first_row, rows) in enumerate(BANDS):
        copies.local(f"r{band}", right_basis.at[pl.ds(first_row, rows), :], r_bands[band].at[y, xl])
    copies.local("g", gradient, g_slots.at[z])
    copies.local("left", left_basis, left)
    copies.local("first", first_moment, first)
    copies.local("second", second_moment, second)

    barrier = pltpu.get_barrier_semaphore()
    peers = [z_up, z_down, y_up, y_down, x_other, sibling] + [target(*d) for d in SPREAD if d != (0, 0)]
    for peer in peers:
        pl.semaphore_signal(barrier, inc=1, device_id=peer, device_id_type=MESH)
    pl.semaphore_wait(barrier, len(peers))

    def pass_g(hop, *strips):
        for strip in strips:
            for way, sign, device in ((0, 1, z_up), (1, -1, z_down)):
                if hop < 3 or strip // 2 == way:
                    copies.wait(f"g{hop - 1}{strip}{way}" if hop else "g")
                    ref = g_slots.at[lax.rem(z - sign * hop + NZ, NZ), :, pl.ds(*G_STRIPS[strip])]
                    copies.start(f"g{hop}{strip}{way}", ref, ref, device)

    def await_g(hop, ways=(0, 1)):
        copies.wait(*(f"g{hop}{strip}{way}" for strip in range(4) for way in ways if hop < 3 or strip // 2 == way))

    routes = {
        "+0": ((0, 0), 0, y_up, None),
        "+1": ((0, 0), 1, y_up, None),
        "-0": ((0, 0), 0, y_down, None),
        "-1": ((0, 0), 1, y_down, None),
        "x0": ((0, 0), 0, x_other, None),
        "x1": ((0, 0), 1, x_other, None),
        "++": ((3, 0), 0, y_up, "+0"),
        "--": ((1, 0), 1, y_down, "-1"),
        "fx1": ((1, 0), 0, x_other, "-0"),
        "fx3": ((3, 0), 0, x_other, "+0"),
        "y+": ((0, 1), 1, y_up, "x1"),
        "y-": ((0, 1), 1, y_down, "x1"),
        "y++": ((3, 1), 1, y_up, "y+"),
        "y--": ((1, 1), 0, y_down, "fx1"),
    }

    def pass_r(band, *names):
        for name in names:
            block, piece, device, after = routes[name]
            copies.wait(f"r{band}" if after is None else f"r{band}{after}")
            ref = r_bands[band].at[(*member(*block), pl.ds(*PIECES[band][piece]))]
            copies.start(f"r{band}{name}", ref, ref, device)

    send_own = pass_r

    def compact(distance):
        slot = lax.rem(z + distance + NZ, NZ)
        g_wide[pl.ds(pl.multiple_of(slot * GROWS, 8), GROWS), :] = g_slots[slot].astype(F32)

    pass_g(0, 0, 2)
    pass_r(0, "+0", "-0", "x1")
    pass_g(0, 1, 3)
    pass_r(0, "+1", "-1", "x0")
    compact(0)
    pass_g(1, 0, 2)
    pass_r(0, "++", "fx1", "y+", "y-", "fx3")
    pass_r(1, "+0", "-0", "x1")
    pass_g(1, 1, 3)
    pass_r(1, "+1", "-1", "x0")
    pass_g(2, 0, 2)
    pass_r(0, "--")
    pass_g(2, 1, 3)
    compact(1)
    compact(-1)
    pass_g(3, 0, 2)
    pass_r(0, "y--")
    pass_g(3, 1, 3)
    compact(2)
    compact(-2)
    pass_r(0, "y++")
    pass_r(1, "fx1", "y+", "y-", "--", "++", "fx3")
    await_g(2)
    compact(3)
    compact(-3)
    await_g(3)
    compact(4)
    g_all[...] = g_wide[...].astype(BF16)

    def left_rows(yy, xx):
        return left[pl.ds(pl.multiple_of((yy * NXL + xx) * BLOCK, 64), BLOCK), :]

    theirs, mine = lax.rem(xl + 1 - core, NXL), lax.rem(xl + core, NXL)

    def right_products(band, keep, give, got):
        rows = BANDS[band][1]
        copies.wait(*(f"r{band}{name}" for name in routes))
        for xx, result in ((theirs, give), (mine, keep)):
            right = r_bands[band][:, xx].reshape(NY * rows, COLS)
            result[...] = lax.dot_general(
                right, g_all[...], (((1,), (1,)), ((), ())), preferred_element_type=F32
            ).reshape(NY, rows, BLOCK)
            if result is give:
                copies.start(f"f{band}c", give, got, sibling)

    def spread(tag, band, dy, keep, got, sent, landed):
        yy = lax.rem(y + dy, NY)
        value = (keep[yy] + got[yy]).astype(BF16)
        sent[yy] = value
        for e in (1, 0):
            only = None
            if (dy, e) == (0, 0):
                only = core == 1

                @pl.when(core == 0)
                def _():
                    landed[y, xl, 0] = value

            copies.start(f"{tag}{band}s{dy}{e}", sent.at[yy], landed.at[y, xl, e], target(dy, e), only)

    def spread_right(band, keep, got, sent, landed):
        copies.wait(f"f{band}c")
        for dy in FAR_FIRST:
            spread("f", band, dy, keep, got, sent, landed)

    def left_products(band, normalized, keep, give, got, sent, landed):
        def product(yy, xx):
            return lax.dot_general(
                normalized, left_rows(yy, xx), (((1,), (1,)), ((), ())), preferred_element_type=F32
            )

        for dy in FAR_FIRST:
            yy = lax.rem(y + dy, NY)
            give[yy] = product(yy, theirs)
            copies.start(f"b{band}c{dy}", give.at[yy], got.at[yy], sibling)
        for dy in FAR_FIRST:
            yy = lax.rem(y + dy, NY)
            keep[yy] = product(yy, mine)
            copies.wait(f"b{band}c{dy}")
            spread("b", band, dy, keep, got, sent, landed)

    def share(tag, band, landed):
        for dy in FAR_FIRST:
            ref = landed.at[lax.rem(y + NY - dy, NY), mine]
            copies.wait(f"{tag}{band}s{dy}1", f"{tag}{band}s{dy}0")
            copies.start(f"{tag}{band}r{dy}", ref, ref, sibling)

    first_fix = 1.0 - beta_first**STEP
    second_fix = 1.0 - beta_second**STEP

    def middle(band, landed):
        first_row, rows = BANDS[band]
        product = jnp.zeros((2 * rows, EIG), F32)
        for xx in (mine, theirs):
            for dy in FAR_FIRST:
                yy = lax.rem(y + NY - dy, NY)
                if xx is theirs:
                    copies.wait(f"f{band}r{dy}")
                product += jnp.dot(
                    landed[yy, xx].reshape(2 * rows, BLOCK), left_rows(yy, xx), preferred_element_type=F32
                )
        rotated = product[:rows] + product[rows:]
        at_rows = pl.ds(first_row, rows)
        copies.wait("first", "second")
        next_first = beta_first * first[at_rows, :] + (1.0 - beta_first) * rotated
        next_second = beta_second * second[at_rows, :] + (1.0 - beta_second) * rotated * rotated
        first_out[at_rows, :] = next_first
        second_out[at_rows, :] = next_second
        return (next_first / first_fix / (jnp.sqrt(next_second / second_fix) + epsilon)).astype(BF16)

    def update_part(band, landed, half):
        rows = BANDS[band][1]
        right = r_bands[band][:, :, :, pl.ds(half * HALF, HALF)].reshape(GROUP * rows, HALF)
        return sum(
            lax.dot_general(
                landed[:, :, i].reshape(GROUP * rows, BLOCK),
                right,
                (((0,), (0,)), ((), ())),
                preferred_element_type=F32,
            )
            for i in (0, 1)
        )

    pass_r(1, "y--")
    right_products(0, keep_top, give_top, got_top)
    pass_r(1, "y++")
    spread_right(0, keep_top, got_top, sent_top, mid_top)
    right_products(1, keep_low, give_low, got_low)
    spread_right(1, keep_low, got_low, sent_low, mid_low)
    share("f", 0, mid_top)
    copies.wait("left")
    normalized = middle(0, mid_top)
    left_products(0, normalized, bkeep_top, bgive_top, bgot_top, bsent_top, end_top)
    share("f", 1, mid_low)
    normalized = middle(1, mid_low)
    left_products(1, normalized, bkeep_low, bgive_low, bgot_low, bsent_low, end_low)
    copies.local("new_first", first_out, new_first)
    copies.local("new_second", second_out, new_second)
    share("b", 0, end_top)
    copies.wait(*(f"b0r{dy}" for dy in FAR_FIRST))
    for half in (0, 1):
        total[:, pl.ds(half * HALF, HALF)] = update_part(0, end_top, half)
    share("b", 1, end_low)
    copies.wait(*(f"b1r{dy}" for dy in FAR_FIRST))
    for half in (0, 1):
        total[:, pl.ds(half * HALF, HALF)] += update_part(1, end_low, half)

    def total_rows(distance, strip):
        rows = lax.rem(z + distance + NZ, NZ) * GROWS
        return total[pl.ds(pl.multiple_of(rows, 8), GROWS), pl.ds(*STRIPS[strip])]

    for step in range(4):
        for strip in (0, 3, 1, 4, 2, 5):
            for way, sign, device in ((0, -1, z_down), (1, 1, z_up)):
                starts = strip // 3 == way
                if step == 0 and not starts:
                    continue
                columns = pl.ds(*STRIPS[strip])
                value = total_rows(sign * (4 - step), strip)
                if step > 1 or (step == 1 and starts):
                    copies.wait(f"u{step - 1}{way}{strip}")
                    value = value + sums_in[way, step - 1, :, columns].astype(F32)
                sums[way, step, :, columns] = value.astype(BF16)
                copies.start(
                    f"u{step}{way}{strip}",
                    sums.at[way, step, :, columns],
                    sums_in.at[way, step, :, columns],
                    device,
                )
    for strip in (0, 3, 1, 4, 2, 5):
        columns = pl.ds(*STRIPS[strip])
        value = total_rows(0, strip)
        for way in (0, 1):
            copies.wait(f"u3{way}{strip}")
            value = value + sums_in[way, 3, :, columns].astype(F32)
        update_out[:, columns] = value
    copies.local("update", update_out, update)
    copies.finish()


COPIES = 28 + 28 + 2 * (1 + 8 + 4) + 2 * (4 + 8 + 4) + 42


def body(gradient, left_basis, right_basis, first_moment, second_moment):
    def bands(*shape, dtype):
        return [pltpu.VMEM((*shape, rows, BLOCK), dtype) for _, rows in BANDS]

    middle = [
        *bands(NY, dtype=F32),
        *bands(NY, dtype=F32),
        *bands(NY, dtype=F32),
        *bands(NY, dtype=BF16),
        *bands(NY, NXL, 2, dtype=BF16),
    ]
    moment = pltpu.VMEM((ROWS, EIG), F32)
    results = pl.pallas_call(
        kernel,
        out_shape=(
            jax.ShapeDtypeStruct((GROWS, COLS), F32),
            jax.ShapeDtypeStruct((ROWS, EIG), F32),
            jax.ShapeDtypeStruct((ROWS, EIG), F32),
        ),
        in_specs=[pl.BlockSpec(memory_space=pl.ANY)] * 5,
        out_specs=[pl.BlockSpec(memory_space=pl.ANY)] * 3,
        scratch_shapes=[
            pltpu.VMEM((NZ, GROWS, COLS), BF16),
            pltpu.VMEM((BLOCK, COLS), F32),
            pltpu.VMEM((BLOCK, COLS), BF16),
            *(pltpu.VMEM((NY, NXL, rows, COLS), BF16) for _, rows in BANDS),
            pltpu.VMEM((GROUP * BLOCK, EIG), BF16),
            *[moment] * 4,
            *middle,
            *middle,
            pltpu.VMEM((BLOCK, COLS), F32),
            pltpu.VMEM((2, 4, GROWS, COLS), BF16),
            pltpu.VMEM((2, 4, GROWS, COLS), BF16),
            pltpu.VMEM((GROWS, COLS), F32),
            pltpu.SemaphoreType.DMA((9,)),
            pltpu.SemaphoreType.DMA((COPIES,)),
            pltpu.SemaphoreType.DMA((COPIES,)),
        ],
        compiler_params=pltpu.CompilerParams(
            collective_id=0, has_side_effects=True, vmem_limit_bytes=56 * 1024 * 1024
        ),
        cost_estimate=pl.CostEstimate(flops=3 * 10**9, bytes_accessed=5 * 10**6, transcendentals=0),
    )(gradient, left_basis, right_basis, first_moment, second_moment)
    return hand_over(results)


def hand_over(results):
    def move(*refs):
        sources, targets, held, sem = refs[:3], refs[3:6], refs[6:9], refs[9]
        loads = [pltpu.make_async_copy(sources[i], held[i], sem.at[i]) for i in range(3)]
        stores = [pltpu.make_async_copy(held[i], targets[i], sem.at[i + 3]) for i in range(3)]
        for one in loads:
            one.start()
        for load, store in zip(loads, stores):
            load.wait()
            store.start()
        for one in stores:
            one.wait()

    return pl.pallas_call(
        move,
        out_shape=tuple(jax.ShapeDtypeStruct(one.shape, one.dtype) for one in results),
        in_specs=[pl.BlockSpec(memory_space=pl.ANY)] * 3,
        out_specs=[pl.BlockSpec(memory_space=pl.ANY)] * 3,
        compiler_params=pltpu.CompilerParams(vmem_limit_bytes=60 * 1024 * 1024),
        scratch_shapes=[
            *(pltpu.VMEM(one.shape, one.dtype) for one in results),
            pltpu.SemaphoreType.DMA((6,)),
        ],
    )(*results)


def solution(mesh):
    return jax.shard_map(
        body,
        mesh=mesh,
        in_specs=(
            P("wide", "narrow"),
            P(None, "narrow"),
            P("wide", "narrow"),
            P("wide", "narrow"),
            P("wide", "narrow"),
        ),
        out_specs=(P("wide", "narrow"), P("wide", "narrow"), P("wide", "narrow")),
        check_vma=False,
    )
```

time: 84.4 us -> 79.4 us (0.941)
  local copies, waits for them, and re-layouts: 5.06 us -> 0 us
    unnamed x3 -> x0, local copies, waits for them, and re-layouts: 5.06 us -> none
    pallas_call x0 -> x1, Pallas kernels: none -> 1.91 us  [hand_over(): pl.pallas_call(move, out_shape=tuple((jax.ShapeDtypeStruct(one.shape, one...]
    pallas_call x1, Pallas kernels: 78.6 us -> 76.8 us  [body(): pl.pallas_call(kernel, out_shape=(jax.ShapeDtypeStruct((GROWS, COLS), F32...]
where the time goes in v3:
time: 79.4 us; the launch traced here: 79.3 us
  Pallas kernels  78.7 us (99%)
    pallas_call x1, Pallas kernels, body(): pl.pallas_call(kernel, out_shape=(jax.ShapeDtypeStruct((GROWS, COLS), F32...  76.8 us
    pallas_call x1, Pallas kernels, hand_over(): pl.pallas_call(move, out_shape=tuple((jax.ShapeDtypeStruct(one.shape, one...  1.91 us

profile of v3, /device:TPU:1, one launch (start us, length us, event | category | flops | bytes accessed | tf_op | source)
XLA Modules:
  0.0 79.3 jit_solution(13368216255383968703)
XLA Ops:
  0.6 76.8 %shard_map.76 = (f32[40,1792]{1,0:T(8,128)}, f32[112,640]{1,0:T(8,128)}, f32[112,640]{1,0:T(8,128)}) custom-call(bf16[40,1792]{1,0:T(8,128)(2,1)} %gradient.1, bf16[2560,640]{1,0:T(8,128)(2,1)} %left_basis.1, bf16[112,1792]{1,0:T(8,128)(2,1)} %right_basis.1, f32[112,640]{1,0:T(8,128)} %first_moment.1, f32[112,640]{1,0:T(8,128)} %second_moment.1), custom_call_target="tpu_custom_call" | custom-call | flops 3000000000 | bytes 5000000 | tf_op jit(solution)/shard_map/pallas_call | solution.py:352
  77.4 1.9 %shard_map.77 = (f32[40,1792]{1,0:T(8,128)}, f32[112,640]{1,0:T(8,128)}, f32[112,640]{1,0:T(8,128)}) custom-call(f32[40,1792]{1,0:T(8,128)} %get-tuple-element.6.refs_0_, f32[112,640]{1,0:T(8,128)} %get-tuple-element.7.refs_1_, f32[112,640]{1,0:T(8,128)} %get-tuple-element.8.refs_2_), custom_call_target="tpu_custom_call" | custom-call | tf_op jit(solution)/shard_map/pallas_call | solution.py:399

commit v4 on v3

--- a/solution.py
+++ b/solution.py
@@ -113,10 +113,11 @@
         pl.semaphore_signal(barrier, inc=1, device_id=peer, device_id_type=MESH)
     pl.semaphore_wait(barrier, len(peers))
 
-    def pass_g(hop, *strips):
-        for strip in strips:
+    def pass_g(hop, *turns):
+        for turn in turns:
             for way, sign, device in ((0, 1, z_up), (1, -1, z_down)):
-                if hop < 3 or strip // 2 == way:
+                strip = (turn + 2 * way) % 4
+                if hop < 3 or turn < 2:
                     copies.wait(f"g{hop - 1}{strip}{way}" if hop else "g")
                     ref = g_slots.at[lax.rem(z - sign * hop + NZ, NZ), :, pl.ds(*G_STRIPS[strip])]
                     copies.start(f"g{hop}{strip}{way}", ref, ref, device)
@@ -154,24 +155,23 @@
         slot = lax.rem(z + distance + NZ, NZ)
         g_wide[pl.ds(pl.multiple_of(slot * GROWS, 8), GROWS), :] = g_slots[slot].astype(F32)
 
-    pass_g(0, 0, 2)
+    pass_g(0, 0, 1)
     pass_r(0, "+0", "-0", "x1")
-    pass_g(0, 1, 3)
+    pass_g(0, 2, 3)
     pass_r(0, "+1", "-1", "x0")
     compact(0)
-    pass_g(1, 0, 2)
+    pass_g(1, 0, 1)
     pass_r(0, "++", "fx1", "y+", "y-", "fx3")
     pass_r(1, "+0", "-0", "x1")
-    pass_g(1, 1, 3)
+    pass_g(1, 2, 3)
     pass_r(1, "+1", "-1", "x0")
-    pass_g(2, 0, 2)
+    pass_g(2, 0, 1)
     pass_r(0, "--")
-    pass_g(2, 1, 3)
+    pass_g(2, 2, 3)
     compact(1)
     compact(-1)
-    pass_g(3, 0, 2)
+    pass_g(3, 0, 1)
     pass_r(0, "y--")
-    pass_g(3, 1, 3)
     compact(2)
     compact(-2)
     pass_r(0, "y++")
@@ -264,17 +264,15 @@
         second_out[at_rows, :] = next_second
         return (next_first / first_fix / (jnp.sqrt(next_second / second_fix) + epsilon)).astype(BF16)
 
-    def update_part(band, landed, half):
+    def update_part(band, landed, xx, half):
         rows = BANDS[band][1]
-        right = r_bands[band][:, :, :, pl.ds(half * HALF, HALF)].reshape(GROUP * rows, HALF)
-        return sum(
-            lax.dot_general(
-                landed[:, :, i].reshape(GROUP * rows, BLOCK),
-                right,
-                (((0,), (0,)), ((), ())),
-                preferred_element_type=F32,
-            )
-            for i in (0, 1)
+        right = r_bands[band][:, xx, :, pl.ds(half * HALF, HALF)]
+        twice = jnp.broadcast_to(right[:, None], (NY, 2, rows, HALF)).reshape(2 * NY * rows, HALF)
+        return lax.dot_general(
+            landed[:, xx].reshape(2 * NY * rows, BLOCK),
+            twice,
+            (((0,), (0,)), ((), ())),
+            preferred_element_type=F32,
         )
 
     pass_r(1, "y--")
@@ -293,13 +291,17 @@
     copies.local("new_first", first_out, new_first)
     copies.local("new_second", second_out, new_second)
     share("b", 0, end_top)
+    for half in (0, 1):
+        total[:, pl.ds(half * HALF, HALF)] = update_part(0, end_top, mine, half)
     copies.wait(*(f"b0r{dy}" for dy in FAR_FIRST))
     for half in (0, 1):
-        total[:, pl.ds(half * HALF, HALF)] = update_part(0, end_top, half)
+        total[:, pl.ds(half * HALF, HALF)] += update_part(0, end_top, theirs, half)
     share("b", 1, end_low)
+    for half in (0, 1):
+        total[:, pl.ds(half * HALF, HALF)] += update_part(1, end_low, mine, half)
     copies.wait(*(f"b1r{dy}" for dy in FAR_FIRST))
     for half in (0, 1):
-        total[:, pl.ds(half * HALF, HALF)] += update_part(1, end_low, half)
+        total[:, pl.ds(half * HALF, HALF)] += update_part(1, end_low, theirs, half)
 
     def total_rows(distance, strip):
         rows = lax.rem(z + distance + NZ, NZ) * GROWS
@@ -334,7 +336,7 @@
     copies.finish()
 
 
-COPIES = 28 + 28 + 2 * (1 + 8 + 4) + 2 * (4 + 8 + 4) + 42
+COPIES = 28 + 28 + 4 * (4 + 8 + 4) + 42
 
 
 def body(gradient, left_basis, right_basis, first_moment, second_moment):

time: 79.4 us -> 77.7 us (0.979)
  Pallas kernels: 78.7 us -> 76.7 us
    pallas_call x1, Pallas kernels: 76.8 us -> 74.8 us  [body(): pl.pallas_call(kernel, out_shape=(jax.ShapeDtypeStruct((GROWS, COLS), F32...]
where the time goes in v4:
time: 77.7 us; the launch traced here: 77.4 us
  Pallas kernels  76.7 us (99%)
    pallas_call x1, Pallas kernels, body(): pl.pallas_call(kernel, out_shape=(jax.ShapeDtypeStruct((GROWS, COLS), F32...  74.8 us
    pallas_call x1, Pallas kernels, hand_over(): pl.pallas_call(move, out_shape=tuple((jax.ShapeDtypeStruct(one.shape, one...  1.91 us

profile of v4, /device:TPU:1, one launch (start us, length us, event | category | flops | bytes accessed | tf_op | source)
XLA Modules:
  0.0 77.4 jit_solution(9561886105576162728)
XLA Ops:
  0.6 74.8 %shard_map.76 = (f32[40,1792]{1,0:T(8,128)}, f32[112,640]{1,0:T(8,128)}, f32[112,640]{1,0:T(8,128)}) custom-call(bf16[40,1792]{1,0:T(8,128)(2,1)} %gradient.1, bf16[2560,640]{1,0:T(8,128)(2,1)} %left_basis.1, bf16[112,1792]{1,0:T(8,128)(2,1)} %right_basis.1, f32[112,640]{1,0:T(8,128)} %first_moment.1, f32[112,640]{1,0:T(8,128)} %second_moment.1), custom_call_target="tpu_custom_call" | custom-call | flops 3000000000 | bytes 5000000 | tf_op jit(solution)/shard_map/pallas_call | solution.py:354
  75.5 1.9 %shard_map.77 = (f32[40,1792]{1,0:T(8,128)}, f32[112,640]{1,0:T(8,128)}, f32[112,640]{1,0:T(8,128)}) custom-call(f32[40,1792]{1,0:T(8,128)} %get-tuple-element.6.refs_0_, f32[112,640]{1,0:T(8,128)} %get-tuple-element.7.refs_1_, f32[112,640]{1,0:T(8,128)} %get-tuple-element.8.refs_2_), custom_call_target="tpu_custom_call" | custom-call | tf_op jit(solution)/shard_map/pallas_call | solution.py:401

commit v5 on v4

--- a/solution.py
+++ b/solution.py
@@ -76,7 +76,7 @@
     g_slots, g_wide, g_all, r_top, r_low, left, first, second, first_out, second_out,
     keep_top, keep_low, give_top, give_low, got_top, got_low, sent_top, sent_low, mid_top, mid_low,
     bkeep_top, bkeep_low, bgive_top, bgive_low, bgot_top, bgot_low, bsent_top, bsent_low, end_top, end_low,
-    total, sums, sums_in, update_out,
+    total, sums, sums_in, last_sums, last_in, update_out,
     local_sem, send_sem, recv_sem,
 ):
     wide, narrow = lax.axis_index("wide"), lax.axis_index("narrow")
@@ -318,11 +318,12 @@
                 if step > 1 or (step == 1 and starts):
                     copies.wait(f"u{step - 1}{way}{strip}")
                     value = value + sums_in[way, step - 1, :, columns].astype(F32)
-                sums[way, step, :, columns] = value.astype(BF16)
+                sent, landed = (last_sums, last_in) if step == 3 else (sums.at[:, step], sums_in.at[:, step])
+                sent[way, :, columns] = value.astype(sent.dtype)
                 copies.start(
                     f"u{step}{way}{strip}",
-                    sums.at[way, step, :, columns],
-                    sums_in.at[way, step, :, columns],
+                    sent.at[way, :, columns],
+                    landed.at[way, :, columns],
                     device,
                 )
     for strip in (0, 3, 1, 4, 2, 5):
@@ -330,9 +331,9 @@
         value = total_rows(0, strip)
         for way in (0, 1):
             copies.wait(f"u3{way}{strip}")
-            value = value + sums_in[way, 3, :, columns].astype(F32)
+            value = value + last_in[way, :, columns]
         update_out[:, columns] = value
-    copies.local("update", update_out, update)
+        copies.local(f"update{strip}", update_out.at[:, columns], update.at[:, columns])
     copies.finish()
 
 
@@ -370,10 +371,12 @@
             *middle,
             *middle,
             pltpu.VMEM((BLOCK, COLS), F32),
-            pltpu.VMEM((2, 4, GROWS, COLS), BF16),
-            pltpu.VMEM((2, 4, GROWS, COLS), BF16),
+            pltpu.VMEM((2, 3, GROWS, COLS), BF16),
+            pltpu.VMEM((2, 3, GROWS, COLS), BF16),
+            pltpu.VMEM((2, GROWS, COLS), F32),
+            pltpu.VMEM((2, GROWS, COLS), F32),
             pltpu.VMEM((GROWS, COLS), F32),
-            pltpu.SemaphoreType.DMA((9,)),
+            pltpu.SemaphoreType.DMA((14,)),
             pltpu.SemaphoreType.DMA((COPIES,)),
             pltpu.SemaphoreType.DMA((COPIES,)),
         ],

time: 77.7 us -> 80.6 us (1.037)
  Pallas kernels: 76.7 us -> 79.8 us
    pallas_call x1, Pallas kernels: 74.8 us -> 77.9 us  [body(): pl.pallas_call(kernel, out_shape=(jax.ShapeDtypeStruct((GROWS, COLS), F32...]
where the time goes in v5:
time: 80.6 us; the launch traced here: 80.5 us
  Pallas kernels  79.8 us (99%)
    pallas_call x1, Pallas kernels, body(): pl.pallas_call(kernel, out_shape=(jax.ShapeDtypeStruct((GROWS, COLS), F32...  77.9 us
    pallas_call x1, Pallas kernels, hand_over(): pl.pallas_call(move, out_shape=tuple((jax.ShapeDtypeStruct(one.shape, one...  1.91 us

profile of v5, /device:TPU:1, one launch (start us, length us, event | category | flops | bytes accessed | tf_op | source)
XLA Modules:
  0.0 80.5 jit_solution(6306680066808033528)
XLA Ops:
  0.6 77.9 %shard_map.76 = (f32[40,1792]{1,0:T(8,128)}, f32[112,640]{1,0:T(8,128)}, f32[112,640]{1,0:T(8,128)}) custom-call(bf16[40,1792]{1,0:T(8,128)(2,1)} %gradient.1, bf16[2560,640]{1,0:T(8,128)(2,1)} %left_basis.1, bf16[112,1792]{1,0:T(8,128)(2,1)} %right_basis.1, f32[112,640]{1,0:T(8,128)} %first_moment.1, f32[112,640]{1,0:T(8,128)} %second_moment.1), custom_call_target="tpu_custom_call" | custom-call | flops 3000000000 | bytes 5000000 | tf_op jit(solution)/shard_map/pallas_call | solution.py:355
  78.6 1.9 %shard_map.77 = (f32[40,1792]{1,0:T(8,128)}, f32[112,640]{1,0:T(8,128)}, f32[112,640]{1,0:T(8,128)}) custom-call(f32[40,1792]{1,0:T(8,128)} %get-tuple-element.6.refs_0_, f32[112,640]{1,0:T(8,128)} %get-tuple-element.7.refs_1_, f32[112,640]{1,0:T(8,128)} %get-tuple-element.8.refs_2_), custom_call_target="tpu_custom_call" | custom-call | tf_op jit(solution)/shard_map/pallas_call | solution.py:404

commit v6 on v4

--- a/solution.py
+++ b/solution.py
@@ -332,7 +332,7 @@
             copies.wait(f"u3{way}{strip}")
             value = value + sums_in[way, 3, :, columns].astype(F32)
         update_out[:, columns] = value
-    copies.local("update", update_out, update)
+        copies.local(f"update{strip}", update_out.at[:, columns], update.at[:, columns])
     copies.finish()
 
 
@@ -373,7 +373,7 @@
             pltpu.VMEM((2, 4, GROWS, COLS), BF16),
             pltpu.VMEM((2, 4, GROWS, COLS), BF16),
             pltpu.VMEM((GROWS, COLS), F32),
-            pltpu.SemaphoreType.DMA((9,)),
+            pltpu.SemaphoreType.DMA((14,)),
             pltpu.SemaphoreType.DMA((COPIES,)),
             pltpu.SemaphoreType.DMA((COPIES,)),
         ],

time: 77.7 us -> 77.7 us (level)
  no operation moved by 1% of the time
where the time goes in v6:
time: 77.7 us; the launch traced here: 77.3 us
  Pallas kernels  76.7 us (99%)
    pallas_call x1, Pallas kernels, body(): pl.pallas_call(kernel, out_shape=(jax.ShapeDtypeStruct((GROWS, COLS), F32...  74.8 us
    pallas_call x1, Pallas kernels, hand_over(): pl.pallas_call(move, out_shape=tuple((jax.ShapeDtypeStruct(one.shape, one...  1.91 us

profile of v6, /device:TPU:1, one launch (start us, length us, event | category | flops | bytes accessed | tf_op | source)
XLA Modules:
  0.0 77.3 jit_solution(16509557151107061041)
XLA Ops:
  0.6 74.8 %shard_map.76 = (f32[40,1792]{1,0:T(8,128)}, f32[112,640]{1,0:T(8,128)}, f32[112,640]{1,0:T(8,128)}) custom-call(bf16[40,1792]{1,0:T(8,128)(2,1)} %gradient.1, bf16[2560,640]{1,0:T(8,128)(2,1)} %left_basis.1, bf16[112,1792]{1,0:T(8,128)(2,1)} %right_basis.1, f32[112,640]{1,0:T(8,128)} %first_moment.1, f32[112,640]{1,0:T(8,128)} %second_moment.1), custom_call_target="tpu_custom_call" | custom-call | flops 3000000000 | bytes 5000000 | tf_op jit(solution)/shard_map/pallas_call | solution.py:354
  75.4 1.9 %shard_map.77 = (f32[40,1792]{1,0:T(8,128)}, f32[112,640]{1,0:T(8,128)}, f32[112,640]{1,0:T(8,128)}) custom-call(f32[40,1792]{1,0:T(8,128)} %get-tuple-element.6.refs_0_, f32[112,640]{1,0:T(8,128)} %get-tuple-element.7.refs_1_, f32[112,640]{1,0:T(8,128)} %get-tuple-element.8.refs_2_), custom_call_target="tpu_custom_call" | custom-call | tf_op jit(solution)/shard_map/pallas_call | solution.py:401
